TPU v7x, 32 devices: a whole 2x2x4 slice. The times are simulated.
32 devices in a mesh: surf: 4 (over y, core), line: 8 (over z, x).
Axes of the slice: x: 2, y: 2, z: 4, core: 2. Of those that a mesh axis runs over, the one named last changes fastest.
Arguments:
- inv_block: bfloat16 [16, 16, 320, 320], P('surf', 'line'), as said below
- couple_block: bfloat16 [16, 16, 320, 320], P('surf', 'line')
- face_block: bfloat16 [16, 16, 320, 320], P('surf', 'line'), may hold values from -0.03125 to 0.03125
- rhs: bfloat16 [16, 16, 320, 64], P('surf', 'line'), may hold values from -0.59765625 to 0.59765625
- adjoint_prev: bfloat16 [16, 16, 320, 64], P('surf', 'line'), may hold values from -6 to 6
- nb_line: int32 [16], P('surf'), may hold values from 0 to 15
- send_list: int32 [4, 4, 4], P('surf'), may hold values from 0 to 7, as said below
- send_count: int32 [4, 4], P('surf'), may hold values from 0 to 4
- recv_list: int32 [4, 4, 4], P('surf'), may hold values from 0 to 7, as said below
Outputs:
- adjoint: bfloat16 [16, 16, 320, 64], P('surf', 'line')
Inputs may be any that keep to these rules, and one draw needn't show every extreme that they name: `send_list`: for every sender s the blocks it sends to all peers are 8 distinct positions; every receiver gets 4 * 2 blocks in all at distinct positions. Each device sends 4 blocks to one peer and none to another. Slots at or past the count are unused. `recv_list`: entries of slots at or past the sender's count are unused. `inv_block`: every block is the identity plus a small perturbation, its rows scaled by per-row factors below one.
All inputs are finite; a program needn't handle non-finite values.
Results may differ from a plain program's by a relative error of at most 0.0013.
Values may be sent and summed in bfloat16 or wider, within the bound.
A program may use at most 320 MiB of HBM per device.

v0:
```python
import jax
import jax.numpy as jnp
from jax import lax
from jax.sharding import PartitionSpec as P

HIGH = lax.Precision.HIGHEST


def passed_along(value, axis, steps):
    count = lax.axis_size(axis)
    first, last = (max(0, -steps), min(count, count - steps))
    return lax.ppermute(value, axis, [(source, source + steps) for source in range(first, last)])


def per_device(
    inv_block,
    couple_block,
    face_block,
    rhs,
    adjoint_prev,
    nb_line,
    send_list,
    send_count,
    recv_list,
):
    lines_here, elems_here, block_size, _ = inv_block.shape
    columns = rhs.shape[3]
    stored = lines_here * elems_here
    stacked = jnp.stack([inv_block, couple_block, face_block], axis=2).reshape(
        stored, 3, block_size, block_size
    )
    rhs_rows = rhs.reshape(stored, block_size, columns)
    picked_rows = send_list[0]
    capacity = picked_rows.shape[1]
    outgoing = stacked[picked_rows]
    outgoing_rhs = rhs_rows[picked_rows]
    outgoing_counts = send_count[0][:, None]
    got_blocks, got_rhs, got_counts = (
        lax.all_to_all(outgoing, "surf", split_axis=0, concat_axis=0, tiled=True),
        lax.all_to_all(outgoing_rhs, "surf", split_axis=0, concat_axis=0, tiled=True),
        lax.all_to_all(outgoing_counts, "surf", split_axis=0, concat_axis=0, tiled=True),
    )
    gathered_piece = lax.all_gather(adjoint_prev, "surf", axis=0, tiled=True)
    row_count = gathered_piece.shape[0]
    wanted = jnp.arange(row_count, dtype=jnp.int32)[None, :]
    selector = (nb_line[:, None] == wanted).astype(jnp.bfloat16)
    neighbors = jnp.einsum(
        "lr,rebk->lebk", selector, gathered_piece, preferred_element_type=jnp.float32
    )
    slot_ids = jnp.arange(capacity, dtype=jnp.int32)[None, :]
    is_valid = slot_ids < got_counts
    targets = jnp.where(is_valid, recv_list[0], stored).reshape(-1)
    placed = (
        jnp.zeros((stored, 3, block_size, block_size), jnp.bfloat16)
        .at[targets]
        .set(got_blocks.reshape(-1, 3, block_size, block_size), mode="drop")
    )
    placed_rhs = (
        jnp.zeros((stored, block_size, columns), jnp.bfloat16)
        .at[targets]
        .set(got_rhs.reshape(-1, block_size, columns), mode="drop")
    )
    placed = placed.reshape(lines_here, elems_here, 3, block_size, block_size)
    inv_moved = placed[:, :, 0]
    couple_moved = placed[:, :, 1]
    face_moved = placed[:, :, 2]
    rhs_moved = placed_rhs.reshape(lines_here, elems_here, block_size, columns)
    neighbor_term = jnp.einsum(
        "lebc,lecd->lebd",
        face_moved,
        neighbors.astype(jnp.bfloat16),
        preferred_element_type=jnp.float32,
    )
    forcing = rhs_moved.astype(jnp.float32) - neighbor_term
    items = (
        jnp.moveaxis(inv_moved, 1, 0),
        jnp.moveaxis(couple_moved, 1, 0),
        jnp.moveaxis(forcing, 1, 0),
    )
    identity_block = jnp.broadcast_to(
        jnp.eye(block_size, dtype=jnp.float32), (lines_here, block_size, block_size)
    )
    zero_fill = jnp.zeros((lines_here, block_size, block_size), jnp.float32)

    def segment_step(state_now, elem_items):
        inv_elem, couple_elem, forcing_elem = elem_items
        drive = jnp.concatenate([forcing_elem, zero_fill], axis=-1)
        drive = drive - jnp.einsum(
            "lbc,lcd->lbd", couple_elem.astype(jnp.float32), state_now, precision=HIGH
        )
        return (
            jnp.einsum("lbc,lcd->lbd", inv_elem.astype(jnp.float32), drive, precision=HIGH),
            None,
        )

    start_state = jnp.concatenate(
        [jnp.zeros((lines_here, block_size, columns), jnp.float32), identity_block], axis=-1
    )
    segment_state, _ = lax.scan(segment_step, start_state, items, reverse=True)
    segment_shift = segment_state[..., :columns]
    segment_map = segment_state[..., columns:]

    def pass_inward(turn_index, incoming_now):
        first_value = segment_shift + jnp.einsum(
            "lbc,lcd->lbd", segment_map, incoming_now, precision=HIGH
        )
        return passed_along(first_value, "line", -1)

    incoming = lax.fori_loop(
        0, lax.axis_size("line") - 1, pass_inward, jnp.zeros_like(segment_shift)
    )

    def sweep_step(carried, elem_items):
        inv_elem, couple_elem, forcing_elem = elem_items
        drive = forcing_elem - jnp.einsum(
            "lbc,lcd->lbd", couple_elem.astype(jnp.float32), carried, precision=HIGH
        )
        swept = jnp.einsum("lbc,lcd->lbd", inv_elem.astype(jnp.float32), drive, precision=HIGH)
        return (swept, swept)

    _, sweep = lax.scan(sweep_step, incoming, items, reverse=True)
    return jnp.moveaxis(sweep, 0, 1).astype(jnp.bfloat16)


def solution(mesh):
    in_specs = (
        P("surf", "line", None, None),
        P("surf", "line", None, None),
        P("surf", "line", None, None),
        P("surf", "line", None, None),
        P("surf", "line", None, None),
        P("surf"),
        P("surf", None, None),
        P("surf", None),
        P("surf", None, None),
    )
    out_specs = P("surf", "line", None, None)
    return jax.shard_map(
        per_device, mesh=mesh, in_specs=in_specs, out_specs=out_specs, check_vma=False
    )
```

profile of v0, /device:TPU:0, one launch (start us, length us, event | category | flops | bytes accessed | tf_op | source)
XLA Modules:
  0.0 364.0 jit_solution(16913972544129573399)
XLA Ops:
  7.9 4.2 %all-to-all-start = ((s32[4,1,1]{2,1,0:T(1,128)}), s32[4,1,1]{2,1,0:T(1,128)S(1)}, u32[]{:S(2)}, u32[]{:S(2)}) async-start(s32[4,1,1]{2,1,0:T(1,128)} %copy.39), calls=%async_computation | async-start | bytes 4096 | tf_op jit(solution)/shard_map/all_to_all | solution.py:41
  19.3 5.9 %pad_maximum_fusion = bf16[8,3,320,320]{3,2,0,1:T(8,128)(2,1)} fusion(bf16[8,1,320,320]{3,2,0,1:T(8,128)(2,1)S(1)} %bitcast.102, bf16[8,1,320,320]{3,2,0,1:T(8,128)(2,1)} %bitcast.103, bf16[8,1,320,320]{3,2,0,1:T(8,128)(2,1)} %bitcast.104), kind=kLoop, calls=%fused_computation.26 | loop fusion | flops 4915200 | bytes 9830400 | tf_op jit(solution)/shard_map/stack | solution.py:29
  25.2 9.1 %gather_fusion = bf16[16,3,320,320]{3,2,1,0:T(8,128)(2,1)} fusion(bf16[8,3,320,320]{3,2,0,1:T(8,128)(2,1)} %pad_maximum_fusion, s32[1024]{0:T(1024)S(1)} %pad_clamp_fusion), kind=kCustom, calls=%fused_computation | custom fusion | bytes 19660864 | tf_op jit(solution)/shard_map/gather | solution.py:35
  34.3 6.3 %all-to-all-start.1 = ((bf16[4,4,3,320,320]{4,3,2,1,0:T(8,128)(2,1)}), bf16[4,4,3,320,320]{4,3,2,1,0:T(8,128)(2,1)}, u32[]{:S(2)}, u32[]{:S(2)}) async-start(bf16[4,4,3,320,320]{4,3,2,1,0:T(8,128)(2,1)} %bitcast.97), calls=%async_computation.1 | async-start | bytes 23592960 | tf_op jit(solution)/shard_map/all_to_all | solution.py:39
  45.4 28.2 %all-gather.2.cloned.1.call-done = bf16[16,2,320,64]{2,3,1,0:T(8,128)(2,1)} async-done(((bf16[4,2,320,64]{2,3,1,0:T(8,128)(2,1)}), bf16[16,2,320,64]{2,3,1,0:T(8,128)(2,1)}) %all-gather.2.cloned.1.call-update) | async-done | bytes 1310736 | tf_op jit(solution)/shard_map/all_gather | solution.py:43
  75.9 102.8 %all-to-all-done.1 = bf16[4,4,3,320,320]{4,3,2,1,0:T(8,128)(2,1)} async-done(((bf16[4,4,3,320,320]{4,3,2,1,0:T(8,128)(2,1)}), bf16[4,4,3,320,320]{4,3,2,1,0:T(8,128)(2,1)}, u32[]{:S(2)}, u32[]{:S(2)}) %all-to-all-start.1) | async-done | bytes 9830432 | tf_op jit(solution)/shard_map/all_to_all | solution.py:39
  182.1 29.9 %scatter_fusion = bf16[8,3,320,320]{3,2,1,0:T(8,128)(2,1)} fusion(bf16[8,3,320,320]{3,2,1,0:T(8,128)(2,1)} %broadcast_in_dim.37, s32[16]{0:T(128)S(1)} %fusion.31, bf16[16,3,320,320]{3,2,1,0:T(8,128)(2,1)} %bitcast.14), kind=kCustom, calls=%fused_computation.2 | custom fusion | bytes 29491264 | tf_op jit(solution)/shard_map/scatter | solution.py:56
  220.4 19.6 %while.40 = (s32[]{:T(128)}, f32[4,320,384]{2,1,0:T(8,128)}, bf16[2,4,320,320]{3,2,1,0:T(8,128)(2,1)}, f32[2,4,320,64]{2,3,0,1:T(8,128)}, bf16[2,4,320,320]{3,2,1,0:T(8,128)(2,1)}, /*index=5*/s32[]{:T(128)}) while((s32[]{:T(128)}, f32[4,320,384]{2,1,0:T(8,128)}, bf16[2,4,320,320]{3,2,1,0:T(8,128)(2,1)}, f32[2,4,320,64]{2,3,0,1:T(8,128)}, ...), condition=%wide.region_3.4_spmd, body=%wide.region_2.3_spmd.sunk | while | flops 3775365120 | bytes 11468893 | solution.py:99
  220.4 3.9 %fusion.52 = f32[4,320,384]{2,1,0:T(8,128)S(1)} fusion(f32[4,320,384]{2,1,0:T(8,128)} %get-tuple-element.437, bf16[2,4,320,320]{3,2,1,0:T(8,128)(2,1)} %get-tuple-element.446, s32[]{:T(128)S(6)} %sub.47), kind=kOutput, calls=%fused_computation.7.clone.1 | convolution fusion | flops 1887436800 | bytes 4915204 | tf_op jit(solution)/shard_map/while/body/eval_jaxpr/lbc,lcd->lbd/dot_general | solution.py:88
  225.6 4.6 %fusion.53 = f32[4,320,384]{2,1,0:T(8,128)} fusion(f32[4,320,384]{2,1,0:T(8,128)S(1)} %fusion.52, f32[4,320,64]{2,1,0:T(8,128)S(1)} %bitcast.96, bf16[2,4,320,320]{3,2,1,0:T(8,128)(2,1)} %get-tuple-element.444, s32[]{:T(128)S(6)} %sub.47), kind=kOutput, calls=%fused_computation.4.clone.1 | convolution fusion | flops 1887928320 | bytes 5242884 | tf_op jit(solution)/shard_map/while/body/eval_jaxpr/lbc,lcd->lbd/dot_general | solution.py:92
  230.2 3.9 %fusion.52 = f32[4,320,384]{2,1,0:T(8,128)S(1)} fusion(f32[4,320,384]{2,1,0:T(8,128)} %get-tuple-element.437, bf16[2,4,320,320]{3,2,1,0:T(8,128)(2,1)} %get-tuple-element.446, s32[]{:T(128)S(6)} %sub.47), kind=kOutput, calls=%fused_computation.7.clone.1 | convolution fusion | flops 1887436800 | bytes 4915204 | tf_op jit(solution)/shard_map/while/body/eval_jaxpr/lbc,lcd->lbd/dot_general | solution.py:88
  235.4 4.6 %fusion.53 = f32[4,320,384]{2,1,0:T(8,128)} fusion(f32[4,320,384]{2,1,0:T(8,128)S(1)} %fusion.52, f32[4,320,64]{2,1,0:T(8,128)S(1)} %bitcast.96, bf16[2,4,320,320]{3,2,1,0:T(8,128)(2,1)} %get-tuple-element.444, s32[]{:T(128)S(6)} %sub.47), kind=kOutput, calls=%fused_computation.4.clone.1 | convolution fusion | flops 1887928320 | bytes 5242884 | tf_op jit(solution)/shard_map/while/body/eval_jaxpr/lbc,lcd->lbd/dot_general | solution.py:92
  245.1 104.3 %while.41 = (s32[]{:T(128)}, f32[4,320,64]{1,2,0:T(8,128)S(1)}, f32[4,320,320]{2,1,0:T(8,128)}, f32[4,320,64]{1,2,0:T(8,128)S(1)}, s32[]{:T(128)}) while((s32[]{:T(128)}, f32[4,320,64]{1,2,0:T(8,128)S(1)}, f32[4,320,320]{2,1,0:T(8,128)}, f32[4,320,64]{1,2,0:T(8,128)S(1)}, s32[]{:T(128)}) %tuple.101), condition=%wide.region_5.6_spmd, body=%wide.region_4.5_spmd.sunk | while | flops 314654720 | bytes 3932261 | solution.py:109
  245.1 3.8 %convolution_add_fusion.2 = f32[4,320,64]{1,2,0:T(8,128)S(1)} fusion(f32[4,320,64]{1,2,0:T(8,128)S(1)} %get-tuple-element.461, f32[4,320,320]{2,1,0:T(8,128)} %get-tuple-element.460, f32[4,320,64]{1,2,0:T(8,128)S(1)} %get-tuple-element.454), kind=kOutput, calls=%fused_computation.16.clone.1 | convolution fusion | flops 314654720 | bytes 2621440 | tf_op jit(solution)/shard_map/while/body/eval_jaxpr/lbc,lcd->lbd/dot_general | solution.py:104
  250.1 11.4 %collective-permute-done = f32[4,320,64]{1,2,0:T(8,128)S(1)} collective-permute-done((f32[4,320,64]{1,2,0:T(8,128)S(1)}, f32[4,320,64]{1,2,0:T(8,128)S(1)}, u32[]{:S(2)}, u32[]{:S(2)}) %collective-permute-start) | collective-permute-done | bytes 327712 | tf_op jit(solution)/shard_map/while/body/eval_jaxpr/ppermute | solution.py:12
  266.4 11.2 %collective-permute-done = f32[4,320,64]{1,2,0:T(8,128)S(1)} collective-permute-done((f32[4,320,64]{1,2,0:T(8,128)S(1)}, f32[4,320,64]{1,2,0:T(8,128)S(1)}, u32[]{:S(2)}, u32[]{:S(2)}) %collective-permute-start) | collective-permute-done | bytes 327712 | tf_op jit(solution)/shard_map/while/body/eval_jaxpr/ppermute | solution.py:12
  277.6 3.6 convolution_add_fusion.2
  282.5 10.3 %collective-permute-done = f32[4,320,64]{1,2,0:T(8,128)S(1)} collective-permute-done((f32[4,320,64]{1,2,0:T(8,128)S(1)}, f32[4,320,64]{1,2,0:T(8,128)S(1)}, u32[]{:S(2)}, u32[]{:S(2)}) %collective-permute-start) | collective-permute-done | bytes 327712 | tf_op jit(solution)/shard_map/while/body/eval_jaxpr/ppermute | solution.py:12
  297.7 9.3 %collective-permute-done = f32[4,320,64]{1,2,0:T(8,128)S(1)} collective-permute-done((f32[4,320,64]{1,2,0:T(8,128)S(1)}, f32[4,320,64]{1,2,0:T(8,128)S(1)}, u32[]{:S(2)}, u32[]{:S(2)}) %collective-permute-start) | collective-permute-done | bytes 327712 | tf_op jit(solution)/shard_map/while/body/eval_jaxpr/ppermute | solution.py:12
  312.0 9.0 %collective-permute-done = f32[4,320,64]{1,2,0:T(8,128)S(1)} collective-permute-done((f32[4,320,64]{1,2,0:T(8,128)S(1)}, f32[4,320,64]{1,2,0:T(8,128)S(1)}, u32[]{:S(2)}, u32[]{:S(2)}) %collective-permute-start) | collective-permute-done | bytes 327712 | tf_op jit(solution)/shard_map/while/body/eval_jaxpr/ppermute | solution.py:12
  321.0 3.6 convolution_add_fusion.2
  325.9 9.3 %collective-permute-done = f32[4,320,64]{1,2,0:T(8,128)S(1)} collective-permute-done((f32[4,320,64]{1,2,0:T(8,128)S(1)}, f32[4,320,64]{1,2,0:T(8,128)S(1)}, u32[]{:S(2)}, u32[]{:S(2)}) %collective-permute-start) | collective-permute-done | bytes 327712 | tf_op jit(solution)/shard_map/while/body/eval_jaxpr/ppermute | solution.py:12
  340.1 9.3 %collective-permute-done = f32[4,320,64]{1,2,0:T(8,128)S(1)} collective-permute-done((f32[4,320,64]{1,2,0:T(8,128)S(1)}, f32[4,320,64]{1,2,0:T(8,128)S(1)}, u32[]{:S(2)}, u32[]{:S(2)}) %collective-permute-start) | collective-permute-done | bytes 327712 | tf_op jit(solution)/shard_map/while/body/eval_jaxpr/ppermute | solution.py:12
  349.4 6.5 %while.42 = (s32[]{:T(128)}, f32[4,320,64]{1,2,0:T(8,128)S(1)}, bf16[2,4,320,64]{2,3,0,1:T(8,128)(2,1)S(1)}, bf16[2,4,320,320]{3,2,1,0:T(8,128)(2,1)}, f32[2,4,3...) while((s32[]{:T(128)}, f32[4,320,64]{1,2,0:T(8,128)S(1)}, ...), condition=%wide.region_7.8_spmd, body=%wide.region_6.7_spmd.sunk | while | flops 629227520 | bytes 10618997 | solution.py:121
  (72 shorter events, 66.0 us)
Async XLA Ops:
  6.5 6.4 %copy-start = (bf16[4,2,320,64]{2,3,1,0:T(8,128)(2,1)S(1)}, bf16[4,2,320,64]{2,3,1,0:T(8,128)(2,1)}, u32[]{:S(2)}) copy-start(bf16[4,2,320,64]{2,3,1,0:T(8,128)(2,1)} %param.18) | copy-start | bytes 983044
  7.9 7.9 %all-to-all-start = ((s32[4,1,1]{2,1,0:T(1,128)}), s32[4,1,1]{2,1,0:T(1,128)S(1)}, u32[]{:S(2)}, u32[]{:S(2)}) async-start(s32[4,1,1]{2,1,0:T(1,128)} %copy.39), calls=%async_computation | async-start | bytes 4096 | tf_op jit(solution)/shard_map/all_to_all | solution.py:41
  12.9 6.4 %copy-start.5 = (bf16[4,2,320,320]{3,2,1,0:T(8,128)(2,1)S(1)}, bf16[4,2,320,320]{3,2,1,0:T(8,128)(2,1)}, u32[]{:S(2)}) copy-start(bf16[4,2,320,320]{3,2,1,0:T(8,128)(2,1)} %param.17) | copy-start | bytes 4915204
  15.8 18.5 %all-to-all-start.2 = ((bf16[4,4,320,64]{2,3,1,0:T(8,128)(2,1)}), bf16[4,4,320,64]{2,3,1,0:T(8,128)(2,1)S(1)}, u32[]{:S(2)}, u32[]{:S(2)}) async-start(bf16[4,4,320,64]{2,3,1,0:T(8,128)(2,1)} %bitcast.19), calls=%async_computation.2 | async-start | bytes 1572864 | tf_op jit(solution)/shard_map/all_to_all | solution.py:40
  34.3 7.1 %copy-start.7 = (s32[1,4,4]{2,1,0:T(4,128)S(1)}, s32[1,4,4]{2,1,0:T(4,128)}, u32[]{:S(2)}) copy-start(s32[1,4,4]{2,1,0:T(4,128)} %param.23) | copy-start | bytes 196
  34.3 144.4 %all-to-all-start.1 = ((bf16[4,4,3,320,320]{4,3,2,1,0:T(8,128)(2,1)}), bf16[4,4,3,320,320]{4,3,2,1,0:T(8,128)(2,1)}, u32[]{:S(2)}, u32[]{:S(2)}) async-start(bf16[4,4,3,320,320]{4,3,2,1,0:T(8,128)(2,1)} %bitcast.97), calls=%async_computation.1 | async-start | bytes 23592960 | tf_op jit(solution)/shard_map/all_to_all | solution.py:39
  40.7 32.9 %all-gather.2.cloned.1.call-start = ((), (), s32[]{:S(2)}) async-start(), calls=%async_computation.3 | async-start | bytes 1966080 | tf_op jit(solution)/shard_map/all_gather | solution.py:43
  44.0 29.5 %copy-start.8 = (s32[4]{0:T(128)S(1)}, s32[4]{0:T(128)}, u32[]{:S(2)}) copy-start(s32[4]{0:T(128)} %param.20) | copy-start | bytes 52
  240.0 3.1 copy-start.2
  243.1 1.9 slice-start
  245.0 104.4 %copy-start.3 = (bf16[2,4,320,320]{3,2,1,0:T(8,128)(2,1)S(1)}, bf16[2,4,320,320]{3,2,1,0:T(8,128)(2,1)}, u32[]{:S(2)}) copy-start(bf16[2,4,320,320]{3,2,1,0:T(8,128)(2,1)} %get-tuple-element.485) | copy-start | bytes 4915204
  248.8 12.7 %collective-permute-start = (f32[4,320,64]{1,2,0:T(8,128)S(1)}, f32[4,320,64]{1,2,0:T(8,128)S(1)}, u32[]{:S(2)}, u32[]{:S(2)}) collective-permute-start(f32[4,320,64]{1,2,0:T(8,128)S(1)} %convolution_add_fusion.2), channel_id=1, source_target_pairs={{1,0},{2,1},{3,2},{4,3},{5,4},{6,5},{7,6},{9,8},{10,9},{11,10},{12... | collective-permute-start | bytes 983048 | tf_op jit(solution)/shard_map/while/body/eval_jaxpr/ppermute | solution.py:12
  265.1 12.5 %collective-permute-start = (f32[4,320,64]{1,2,0:T(8,128)S(1)}, f32[4,320,64]{1,2,0:T(8,128)S(1)}, u32[]{:S(2)}, u32[]{:S(2)}) collective-permute-start(f32[4,320,64]{1,2,0:T(8,128)S(1)} %convolution_add_fusion.2), channel_id=1, source_target_pairs={{1,0},{2,1},{3,2},{4,3},{5,4},{6,5},{7,6},{9,8},{10,9},{11,10},{12... | collective-permute-start | bytes 983048 | tf_op jit(solution)/shard_map/while/body/eval_jaxpr/ppermute | solution.py:12
  281.2 11.6 %collective-permute-start = (f32[4,320,64]{1,2,0:T(8,128)S(1)}, f32[4,320,64]{1,2,0:T(8,128)S(1)}, u32[]{:S(2)}, u32[]{:S(2)}) collective-permute-start(f32[4,320,64]{1,2,0:T(8,128)S(1)} %convolution_add_fusion.2), channel_id=1, source_target_pairs={{1,0},{2,1},{3,2},{4,3},{5,4},{6,5},{7,6},{9,8},{10,9},{11,10},{12... | collective-permute-start | bytes 983048 | tf_op jit(solution)/shard_map/while/body/eval_jaxpr/ppermute | solution.py:12
  296.4 10.6 %collective-permute-start = (f32[4,320,64]{1,2,0:T(8,128)S(1)}, f32[4,320,64]{1,2,0:T(8,128)S(1)}, u32[]{:S(2)}, u32[]{:S(2)}) collective-permute-start(f32[4,320,64]{1,2,0:T(8,128)S(1)} %convolution_add_fusion.2), channel_id=1, source_target_pairs={{1,0},{2,1},{3,2},{4,3},{5,4},{6,5},{7,6},{9,8},{10,9},{11,10},{12... | collective-permute-start | bytes 983048 | tf_op jit(solution)/shard_map/while/body/eval_jaxpr/ppermute | solution.py:12
  310.7 10.3 %collective-permute-start = (f32[4,320,64]{1,2,0:T(8,128)S(1)}, f32[4,320,64]{1,2,0:T(8,128)S(1)}, u32[]{:S(2)}, u32[]{:S(2)}) collective-permute-start(f32[4,320,64]{1,2,0:T(8,128)S(1)} %convolution_add_fusion.2), channel_id=1, source_target_pairs={{1,0},{2,1},{3,2},{4,3},{5,4},{6,5},{7,6},{9,8},{10,9},{11,10},{12... | collective-permute-start | bytes 983048 | tf_op jit(solution)/shard_map/while/body/eval_jaxpr/ppermute | solution.py:12
  324.6 10.6 %collective-permute-start = (f32[4,320,64]{1,2,0:T(8,128)S(1)}, f32[4,320,64]{1,2,0:T(8,128)S(1)}, u32[]{:S(2)}, u32[]{:S(2)}) collective-permute-start(f32[4,320,64]{1,2,0:T(8,128)S(1)} %convolution_add_fusion.2), channel_id=1, source_target_pairs={{1,0},{2,1},{3,2},{4,3},{5,4},{6,5},{7,6},{9,8},{10,9},{11,10},{12... | collective-permute-start | bytes 983048 | tf_op jit(solution)/shard_map/while/body/eval_jaxpr/ppermute | solution.py:12
  338.8 10.6 %collective-permute-start = (f32[4,320,64]{1,2,0:T(8,128)S(1)}, f32[4,320,64]{1,2,0:T(8,128)S(1)}, u32[]{:S(2)}, u32[]{:S(2)}) collective-permute-start(f32[4,320,64]{1,2,0:T(8,128)S(1)} %convolution_add_fusion.2), channel_id=1, source_target_pairs={{1,0},{2,1},{3,2},{4,3},{5,4},{6,5},{7,6},{9,8},{10,9},{11,10},{12... | collective-permute-start | bytes 983048 | tf_op jit(solution)/shard_map/while/body/eval_jaxpr/ppermute | solution.py:12
  349.4 2.2 copy-start.4
  352.7 2.2 copy-start.4
  356.0 0.7 copy-start.6
  356.0 1.1 copy-start.1
Sparse Core Ops, SparseCore 0:
  43.1 30.4 all-gather.1
where the time goes:
time: 366 us; the launch traced here: 364 us
  waiting for transfers between devices  203 us (55%)
  local copies, waits for them, and re-layouts  64.5 us (18%)
  matrix products  53 us (14%)
  starting transfers between devices  23.1 us (6%)
  between operations  13.6 us (4%)
  other arithmetic  6.84 us (2%)
    all_to_all x1, waiting for transfers between devices, per_device(): lax.all_to_all(outgoing, 'surf', split_axis=0, concat_axis=0, tiled=True)  103 us
    ppermute x7, waiting for transfers between devices, passed_along(): lax.ppermute(value, axis, [(source, source + steps) for source in range(f...  69.7 us
    scatter x2, local copies, waits for them, and re-layouts, per_device(): placed = jnp.zeros((stored, 3, block_size, block_size), jnp.bfloat16).at[...  33.2 us
    all_gather x1, waiting for transfers between devices, per_device(): gathered_piece = lax.all_gather(adjoint_prev, 'surf', axis=0, tiled=True)  28.2 us
    dot_general x7, matrix products, pass_inward(): jnp.einsum('lbc,lcd->lbd', segment_map, incoming_now, precision=HIGH)  25.4 us
    dot_general x2, matrix products, segment_step(): jnp.einsum('lbc,lcd->lbd', inv_elem.astype(jnp.float32), drive, precision...  9.22 us
    gather x1, local copies, waits for them, and re-layouts, per_device(): outgoing = stacked[picked_rows]  9.13 us
    ppermute x7, starting transfers between devices, passed_along(): lax.ppermute(value, axis, [(source, source + steps) for source in range(f...  9.04 us
  transfers between devices with their start and end apart: 11, of which 10 were waited for; matrix products, arithmetic and copies ran while one was open for 6% of the time, Pallas kernels for 0%

commit v1 on v0

v1 whole, which is shorter than its diff:
```python
import functools

import jax
import jax.numpy as jnp
from jax import lax
from jax.experimental import pallas as pl
from jax.experimental.pallas import tpu as pltpu
from jax.sharding import PartitionSpec as P

MESH = pl.DeviceIdType.MESH
F32 = jnp.float32
BF16 = jnp.bfloat16


def dot(a, b):
    return jnp.dot(a, b, preferred_element_type=F32)


def split(value):
    high = value.astype(BF16)
    return high, (value - high.astype(F32)).astype(BF16)


def line_kernel(
    n, lines, elems, slot_ref, blocks_ref, forcing_ref, out_ref,
    first_hi, first_lo, map_hi, map_lo, first_shift, shift, going, coming, send_sem, recv_sem,
):
    me = lax.axis_index("line")
    size = blocks_ref.shape[1]
    cols = forcing_ref.shape[2] // 2
    inner, outer = jnp.maximum(me - 1, 0), jnp.minimum(me + 1, n - 1)
    barrier = pltpu.get_barrier_semaphore()

    @pl.when(me < n - 1)
    def _():
        pl.semaphore_signal(barrier, inc=1, device_id={"line": outer}, device_id_type=MESH)

    @pl.when(me > 0)
    def _():
        pl.semaphore_wait(barrier, 1)

    def segment(l, _):
        outside, inside = slot_ref[l * elems + 1], slot_ref[l * elems]
        pair = blocks_ref[outside]
        inv, couple = pair[:, :size], pair[:, size:]
        force = forcing_ref[outside]
        a_hi, a_lo = split(-dot(inv, couple))
        moved = dot(inv, force)
        moved = moved[:, :cols] + moved[:, cols:]
        first_hi[l] = a_hi
        first_lo[l] = a_lo
        first_shift[l] = moved
        f_hi, f_lo = split(moved)
        pair = blocks_ref[inside]
        inv, couple = pair[:, :size], pair[:, size:]
        force = forcing_ref[inside].astype(F32)
        force = force[:, :cols] + force[:, cols:]
        d_hi, d_lo = split(-(dot(couple, a_hi) + dot(couple, a_lo)))
        g_hi, g_lo = split(force - (dot(couple, f_hi) + dot(couple, f_lo)))
        m_hi, m_lo = split(dot(inv, d_hi) + dot(inv, d_lo))
        map_hi[l] = m_hi
        map_lo[l] = m_lo
        shift[l] = dot(inv, g_hi) + dot(inv, g_lo)
        return 0

    lax.fori_loop(0, lines, segment, 0)

    def copy(l):
        return pltpu.make_async_remote_copy(
            src_ref=going.at[l], dst_ref=coming.at[l], send_sem=send_sem.at[l],
            recv_sem=recv_sem.at[l], device_id={"line": inner}, device_id_type=MESH,
        )

    @pl.when(me == n - 1)
    def _():
        coming[...] = jnp.zeros_like(coming)

    def applied(hi, lo, value):
        both = dot(hi, value)
        return both[:, :cols] + (both[:, cols:] + dot(lo, value[:, :cols]))

    for l in range(lines):
        @pl.when(me < n - 1)
        def _():
            copy(l).wait_recv()

        last = shift[l] + applied(map_hi[l], map_lo[l], coming[l])
        hi, lo = split(last)
        going[l] = jnp.concatenate([hi, lo], axis=-1)

        @pl.when(me > 0)
        def _():
            copy(l).start()

        out_ref[l, 0] = hi

    for l in range(lines):
        value = first_shift[l] + applied(first_hi[l], first_lo[l], coming[l])
        out_ref[l, 1] = value.astype(BF16)

    for l in range(lines):
        @pl.when(me > 0)
        def _():
            copy(l).wait_send()


def swept(n, lines, elems, slots, blocks, forcing):
    size, cols = blocks.shape[1], forcing.shape[2] // 2
    vmem = pl.BlockSpec(memory_space=pltpu.VMEM)
    square = pltpu.VMEM((lines, size, size), BF16)
    return pl.pallas_call(
        functools.partial(line_kernel, n, lines, elems),
        out_shape=jax.ShapeDtypeStruct((lines, elems, size, cols), BF16),
        in_specs=[pl.BlockSpec(memory_space=pltpu.SMEM), vmem, vmem],
        out_specs=vmem,
        scratch_shapes=[
            square, square, square, square,
            pltpu.VMEM((lines, size, cols), F32),
            pltpu.VMEM((lines, size, cols), F32),
            pltpu.VMEM((lines, size, 2 * cols), BF16),
            pltpu.VMEM((lines, size, 2 * cols), BF16),
            pltpu.SemaphoreType.DMA((lines,)),
            pltpu.SemaphoreType.DMA((lines,)),
        ],
        compiler_params=pltpu.CompilerParams(
            collective_id=0, has_side_effects=True, vmem_limit_bytes=48 << 20
        ),
    )(slots, blocks, forcing)


def pack_kernel(pick_ref, inv_ref, couple_ref, out_ref):
    size = inv_ref.shape[2]
    out_ref[0, :, :size] = inv_ref[0, 0]
    out_ref[0, :, size:] = couple_ref[0, 0]


def packed(picks, inv_block, couple_block):
    _, elems, size, _ = inv_block.shape
    count = picks.shape[0]
    block = pl.BlockSpec(
        (1, 1, size, size), lambda s, pick: (pick[s] // elems, pick[s] % elems, 0, 0)
    )
    return pl.pallas_call(
        pack_kernel,
        out_shape=jax.ShapeDtypeStruct((count, size, 2 * size), BF16),
        grid_spec=pltpu.PrefetchScalarGridSpec(
            num_scalar_prefetch=1,
            grid=(count,),
            in_specs=[block, block],
            out_specs=pl.BlockSpec((1, size, 2 * size), lambda s, pick: (s, 0, 0)),
        ),
        cost_estimate=pl.CostEstimate(
            flops=0, bytes_accessed=8 * count * size * size, transcendentals=0
        ),
    )(picks, inv_block, couple_block)


def force_kernel(elems, pick_ref, line_ref, elem_ref, face_ref, rhs_ref, adjoint_ref, out_ref):
    cols = rhs_ref.shape[3]
    terms = dot(face_ref[0, 0], adjoint_ref[0])
    elem = elem_ref[pl.program_id(0)]
    term = terms[:, :cols]
    for e in range(1, elems):
        term = jnp.where(elem == e, terms[:, e * cols : (e + 1) * cols], term)
    hi, lo = split(rhs_ref[0, 0].astype(F32) - term)
    out_ref[0] = jnp.concatenate([hi, lo], axis=-1)


def forced(picks, lines, elem, face_block, rhs, adjoints):
    _, elems, size, _ = face_block.shape
    cols = rhs.shape[3]
    count = picks.shape[0]

    def stored_at(s, pick, line, elem):
        return (pick[s] // elems, pick[s] % elems, 0, 0)

    return pl.pallas_call(
        functools.partial(force_kernel, elems),
        out_shape=jax.ShapeDtypeStruct((count, size, 2 * cols), BF16),
        grid_spec=pltpu.PrefetchScalarGridSpec(
            num_scalar_prefetch=3,
            grid=(count,),
            in_specs=[
                pl.BlockSpec((1, 1, size, size), stored_at),
                pl.BlockSpec((1, 1, size, cols), stored_at),
                pl.BlockSpec((1, size, elems * cols), lambda s, pick, line, elem: (line[s], 0, 0)),
            ],
            out_specs=pl.BlockSpec((1, size, 2 * cols), lambda s, pick, line, elem: (s, 0, 0)),
        ),
        cost_estimate=pl.CostEstimate(
            flops=4 * count * size * size * cols, bytes_accessed=2 * count * size * size,
            transcendentals=0,
        ),
    )(picks, lines, elem, face_block, rhs, adjoints)


def per_device(n_surf, n_line, inv_block, couple_block, face_block, rhs, adjoint_prev,
               nb_line, send_list, send_count, recv_list):
    lines, elems, size, _ = inv_block.shape
    cols = rhs.shape[3]
    stored = lines * elems
    cap = send_list.shape[2]
    total = n_surf * cap
    me = lax.axis_index("surf")
    ids = jnp.arange(cap, dtype=jnp.int32)[None, :]
    ranks = jnp.arange(n_surf, dtype=jnp.int32)

    leaves = ids < send_count[0][:, None]
    picks = jnp.where(leaves, send_list[0], 0).reshape(-1)
    got_blocks = lax.all_to_all(
        packed(picks, inv_block, couple_block).reshape(n_surf, cap, size, 2 * size),
        "surf", split_axis=0, concat_axis=0, tiled=True,
    )

    table = jnp.concatenate([recv_list[0].reshape(-1), nb_line, send_count[0]])
    tables = lax.all_gather(table, "surf", axis=0, tiled=False)
    places = tables[:, : n_surf * cap].reshape(n_surf, n_surf, cap)
    nb_all = tables[:, n_surf * cap : n_surf * cap + lines].reshape(-1)
    counts = tables[:, n_surf * cap + lines :]

    mine = jnp.sum(jnp.where((ranks == me)[None, :, None], places, 0), axis=1)
    goal = jnp.where(leaves, mine + ranks[:, None] * stored, 0).reshape(-1)
    goal_line, goal_elem = goal // elems, goal % elems
    all_lines = jnp.arange(n_surf * lines, dtype=jnp.int32)
    nb = jnp.sum(jnp.where(goal_line[:, None] == all_lines[None], nb_all[None], 0), axis=1)

    lanes = jnp.concatenate([adjoint_prev[:, e] for e in range(elems)], axis=-1)
    adjoints = lax.all_gather(lanes, "surf", axis=0, tiled=True)
    halves = forced(picks, nb, goal_elem, face_block, rhs, adjoints)
    got_forcing = lax.all_to_all(
        halves.reshape(n_surf, cap, size, 2 * cols), "surf", split_axis=0, concat_axis=0, tiled=True
    )

    to_me = jnp.sum(jnp.where((ranks == me)[None], counts, 0), axis=1)
    valid = (ids < to_me[:, None]).reshape(-1)
    positions = jnp.arange(stored, dtype=jnp.int32)
    hits = (recv_list[0].reshape(-1)[None] == positions[:, None]) & valid[None]
    slots = jnp.sum(jnp.where(hits, jnp.arange(total, dtype=jnp.int32)[None], 0), axis=1)

    return swept(
        n_line, lines, elems, slots,
        got_blocks.reshape(total, size, 2 * size),
        got_forcing.reshape(total, size, 2 * cols),
    )


def solution(mesh):
    whole = P("surf", "line", None, None)
    in_specs = (
        whole, whole, whole, whole, whole,
        P("surf"), P("surf", None, None), P("surf", None), P("surf", None, None),
    )
    body = functools.partial(per_device, mesh.shape["surf"], mesh.shape["line"])
    return jax.shard_map(
        body, mesh=mesh, in_specs=in_specs, out_specs=whole, check_vma=False
    )
```

time: 366 us -> 199 us (0.54)
  waiting for transfers between devices: 203 us -> 86.9 us
  Pallas kernels: 0 us -> 73.6 us
  local copies, waits for them, and re-layouts: 64.5 us -> 5.12 us
  matrix products: 53 us -> 0 us
  starting transfers between devices: 23.1 us -> 8.87 us
  blocking collectives: 0 us -> 6.38 us
    pallas_call x0 -> x3, Pallas kernels: none -> 73.6 us  [the longest x1 47.2 us: swept(): pl.pallas_call(functools.partial(line_kernel, n, lines, elems), out_shape...]
    ppermute x7 -> x0, waiting for transfers between devices: 69.7 us -> none  [passed_along(): lax.ppermute(value, axis, [(source, source + steps) for source in range(f...]
    dot_general x17 -> x0, matrix products: 53 us -> none  [the longest x7 25.4 us: pass_inward(): jnp.einsum('lbc,lcd->lbd', segment_map, incoming_now, precision=HIGH)]
    scatter x3 -> x0, local copies, waits for them, and re-layouts: 34.5 us -> none  [the longest x2 33.2 us: per_device(): placed = jnp.zeros((stored, 3, block_size, block_size), jnp.bfloat16).at[...]
    all_to_all x3 -> x2, waiting for transfers between devices: 104 us -> 77.8 us  [the longest x1 73.2 us: per_device(): lax.all_to_all(packed(picks, inv_block, couple_block).reshape(n_surf, cap...]
    all_gather x1, waiting for transfers between devices: 28.2 us -> 9.15 us  [per_device(): adjoints = lax.all_gather(lanes, 'surf', axis=0, tiled=True)]
    gather x2 -> x0, local copies, waits for them, and re-layouts: 10.7 us -> none  [the longest x1 9.13 us: per_device(): outgoing = stacked[picked_rows]]
    ppermute x7 -> x0, starting transfers between devices: 9.04 us -> none  [passed_along(): lax.ppermute(value, axis, [(source, source + steps) for source in range(f...]
  transfers between devices with their start and end apart: 11 -> 3, of which waited for: 10 -> 3; matrix products, arithmetic and copies ran while one was open for 6% -> 3% of each run, Pallas kernels for 0% -> 6%
where the time goes in v1:
time: 199 us
  waiting for transfers between devices  86.9 us (44%)
  Pallas kernels  73.6 us (37%)
  between operations  14.1 us (7%)
  starting transfers between devices  8.87 us (4%)
  blocking collectives  6.38 us (3%)
  local copies, waits for them, and re-layouts  5.12 us (3%)
  other arithmetic  3.63 us (2%)
    all_to_all x1, waiting for transfers between devices, per_device(): lax.all_to_all(packed(picks, inv_block, couple_block).reshape(n_surf, cap...  73.2 us
    pallas_call x1, Pallas kernels, swept(): pl.pallas_call(functools.partial(line_kernel, n, lines, elems), out_shape...  47.2 us
    pallas_call x1, Pallas kernels, forced(): pl.pallas_call(functools.partial(force_kernel, elems), out_shape=jax.Shap...  13.7 us
    pallas_call x1, Pallas kernels, packed(): pl.pallas_call(pack_kernel, out_shape=jax.ShapeDtypeStruct((count, size,...  12.7 us
    all_gather x1, waiting for transfers between devices, per_device(): adjoints = lax.all_gather(lanes, 'surf', axis=0, tiled=True)  9.15 us
    unnamed x1, blocking collectives  6.38 us
    all_to_all x1, starting transfers between devices, per_device(): lax.all_to_all(packed(picks, inv_block, couple_block).reshape(n_surf, cap...  5.3 us
    all_to_all x1, waiting for transfers between devices, per_device(): lax.all_to_all(halves.reshape(n_surf, cap, size, 2 * cols), 'surf', split...  4.55 us
  transfers between devices with their start and end apart: 3, of which 3 were waited for; matrix products, arithmetic and copies ran while one was open for 3% of the time, Pallas kernels for 6%

profile of v1, /device:TPU:0, one launch (start us, length us, event | category | flops | bytes accessed | tf_op | source)
XLA Modules:
  0.0 198.6 jit_solution(17789159512876358601)
XLA Ops:
  6.6 1.2 fusion.1
  7.8 0.2 copy.23
  8.0 0.2 copy.22
  8.2 0.9 pad_maximum_fusion
  9.3 0.6 dynamic-slice
  10.5 0.2 add_dynamic-update-slice_fusion
  10.7 6.4 %all-reduce = s32[96]{0:T(128)S(1)} all-reduce(s32[96]{0:T(128)S(1)} %add_dynamic-update-slice_fusion), channel_id=2, replica_groups=mesh['surf'=4,'line'=8] {'surf'}, use_global_device_ids=true, to_apply=%add | all-reduce | flops 96 | bytes 768
  17.2 0.1 lt.55
  17.4 0.1 select_reduce_fusion.1
  17.7 0.2 fusion.2
  18.0 1.2 copy.20.rhs_ref
  19.2 0.6 and_select_fusion
  19.7 0.6 and_select_fusion.1
  20.3 0.8 select_reduce_fusion.line_ref
  21.1 9.2 %all-gather.3.cloned.1.call-done.adjoint_ref = bf16[16,320,128]{2,1,0:T(8,128)(2,1)} async-done(((bf16[4,320,128]{2,1,0:T(8,128)(2,1)}), bf16[16,320,128]{2,1,0:T(8,128)(2,1)}) %all-gather.3.cloned.1.call-update) | async-done | bytes 1310736 | tf_op jit(solution)/shard_map/all_gather | solution.py:228
  30.2 13.7 %shard_map.92 = bf16[16,320,128]{2,1,0:T(8,128)(2,1)} custom-call(s32[16]{0:T(128)} %get-tuple-element.12.pick_ref, s32[16]{0:T(128)} %select_reduce_fusion.line_ref, s32[16]{0:T(128)} %get-tuple-element.5.elem_ref, bf16[4,2,320,320]{3,2,1,0:T(8,128)(2,1)} %face_ref.1, bf16[4,2,320,64]{3,2,1,0:T(8,128)(2,1)} %copy.20.rhs_ref, ...), custom_call_target="tpu_custom_call" | custom-call | flops 419430400 | bytes 3276800 | tf_op jit(solution)/shard_map/pallas_call | solution.py:177
  43.9 3.5 %all-to-all-start.1 = ((bf16[4,4,320,128]{3,2,1,0:T(8,128)(2,1)}), bf16[4,4,320,128]{3,2,1,0:T(8,128)(2,1)S(1)}, u32[]{:S(2)}, u32[]{:S(2)}) async-start(bf16[4,4,320,128]{3,2,1,0:T(8,128)(2,1)} %bitcast.11), calls=%async_computation.1 | async-start | bytes 2621440 | tf_op jit(solution)/shard_map/all_to_all | solution.py:230
  47.5 12.7 %shard_map.91 = bf16[16,320,640]{2,1,0:T(8,128)(2,1)} custom-call(s32[16]{0:T(128)} %get-tuple-element.12.pick_ref, bf16[4,2,320,320]{3,2,1,0:T(8,128)(2,1)} %inv_ref.1, bf16[4,2,320,320]{3,2,1,0:T(8,128)(2,1)} %couple_ref.1), custom_call_target="tpu_custom_call" | custom-call | bytes 13107200 | tf_op jit(solution)/shard_map/pallas_call | solution.py:143
  60.2 4.5 %all-to-all-done.1 = bf16[4,4,320,128]{3,2,1,0:T(8,128)(2,1)S(1)} async-done(((bf16[4,4,320,128]{3,2,1,0:T(8,128)(2,1)}), bf16[4,4,320,128]{3,2,1,0:T(8,128)(2,1)S(1)}, u32[]{:S(2)}, u32[]{:S(2)}) %all-to-all-start.1) | async-done | bytes 1310752 | tf_op jit(solution)/shard_map/all_to_all | solution.py:230
  64.7 5.3 %all-to-all-start = ((bf16[4,4,320,640]{3,2,1,0:T(8,128)(2,1)}), bf16[4,4,320,640]{3,2,1,0:T(8,128)(2,1)}, u32[]{:S(2)}, u32[]{:S(2)}) async-start(bf16[4,4,320,640]{3,2,1,0:T(8,128)(2,1)} %bitcast.10), calls=%async_computation | async-start | bytes 13107200 | tf_op jit(solution)/shard_map/all_to_all | solution.py:210
  70.2 0.1 select_reduce_fusion.2.slot_ref
  70.3 73.2 %all-to-all-done = bf16[4,4,320,640]{3,2,1,0:T(8,128)(2,1)} async-done(((bf16[4,4,320,640]{3,2,1,0:T(8,128)(2,1)}), bf16[4,4,320,640]{3,2,1,0:T(8,128)(2,1)}, u32[]{:S(2)}, u32[]{:S(2)}) %all-to-all-start) | async-done | bytes 6553632 | tf_op jit(solution)/shard_map/all_to_all | solution.py:210
  143.5 47.2 %shard_map.93 = bf16[4,2,320,64]{3,2,1,0:T(8,128)(2,1)S(1)} custom-call(s32[8]{0:T(128)S(1)} %select_reduce_fusion.2.slot_ref, bf16[16,320,640]{2,1,0:T(8,128)(2,1)} %bitcast.3.blocks_ref, bf16[16,320,128]{2,1,0:T(8,128)(2,1)S(1)} %bitcast.9), custom_call_target="tpu_custom_call" | custom-call | tf_op jit(solution)/shard_map/pallas_call | solution.py:111
  190.7 1.0 copy.21
  (27 shorter events, 0.9 us)
Async XLA Ops:
  6.5 2.8 %copy-start.5 = (u32[32]{0:T(128)S(1)}, u32[32]{0:T(128)}, u32[]{:S(2)}) copy-start(u32[32]{0:T(128)} %constant.44) | copy-start | bytes 388
  6.5 2.7 %copy-start.1 = (s32[1,4,4]{2,1,0:T(4,128)S(1)}, s32[1,4,4]{2,1,0:T(4,128)}, u32[]{:S(2)}) copy-start(s32[1,4,4]{2,1,0:T(4,128)} %param.17) | copy-start | bytes 196
  6.5 3.9 %copy-start.4 = (s32[1,4]{1,0:T(1,128)S(1)}, s32[1,4]{1,0:T(1,128)}, u32[]{:S(2)}) copy-start(s32[1,4]{1,0:T(1,128)} %param.16) | copy-start | bytes 52
  6.5 3.9 %copy-start.3 = (s32[4]{0:T(128)S(1)}, s32[4]{0:T(128)}, u32[]{:S(2)}) copy-start(s32[4]{0:T(128)} %param.14) | copy-start | bytes 52
  6.5 11.1 %copy-start.2 = (s32[1,4,4]{2,1,0:T(4,128)S(1)}, s32[1,4,4]{2,1,0:T(4,128)}, u32[]{:S(2)}) copy-start(s32[1,4,4]{2,1,0:T(4,128)} %param.15) | copy-start | bytes 196
  6.5 11.4 %copy-start = (bf16[4,2,320,64]{2,3,1,0:T(8,128)(2,1)S(1)}, bf16[4,2,320,64]{2,3,1,0:T(8,128)(2,1)}, u32[]{:S(2)}) copy-start(bf16[4,2,320,64]{2,3,1,0:T(8,128)(2,1)} %param.12) | copy-start | bytes 983044
  6.6 23.7 %all-gather.3.cloned.1.call-start = ((), (), s32[]{:S(2)}) async-start(), calls=%async_computation.2 | async-start | bytes 1638400 | tf_op jit(solution)/shard_map/all_gather | solution.py:228
  43.9 20.8 %all-to-all-start.1 = ((bf16[4,4,320,128]{3,2,1,0:T(8,128)(2,1)}), bf16[4,4,320,128]{3,2,1,0:T(8,128)(2,1)S(1)}, u32[]{:S(2)}, u32[]{:S(2)}) async-start(bf16[4,4,320,128]{3,2,1,0:T(8,128)(2,1)} %bitcast.11), calls=%async_computation.1 | async-start | bytes 2621440 | tf_op jit(solution)/shard_map/all_to_all | solution.py:230
  64.7 78.8 %all-to-all-start = ((bf16[4,4,320,640]{3,2,1,0:T(8,128)(2,1)}), bf16[4,4,320,640]{3,2,1,0:T(8,128)(2,1)}, u32[]{:S(2)}, u32[]{:S(2)}) async-start(bf16[4,4,320,640]{3,2,1,0:T(8,128)(2,1)} %bitcast.10), calls=%async_computation | async-start | bytes 13107200 | tf_op jit(solution)/shard_map/all_to_all | solution.py:210
Sparse Core Ops, SparseCore 0:
  9.3 20.8 all-gather.2

commit v2 on v1

--- a/solution.py
+++ b/solution.py
@@ -22,12 +22,22 @@
 
 
 def line_kernel(
-    n, lines, elems, slot_ref, blocks_ref, forcing_ref, out_ref,
-    first_hi, first_lo, map_hi, map_lo, first_shift, shift, going, coming, send_sem, recv_sem,
+    n, lines, elems, n_slabs, slot_ref, *refs
 ):
+    blocks, forces, rest = refs[:n_slabs], refs[n_slabs : 2 * n_slabs], refs[2 * n_slabs :]
+    (out_ref, first_hi, first_lo, map_hi, map_lo, first_shift, shift, going, coming,
+     send_sem, recv_sem) = rest
     me = lax.axis_index("line")
-    size = blocks_ref.shape[1]
-    cols = forcing_ref.shape[2] // 2
+    cap, size, _ = blocks[0].shape
+    cols = forces[0].shape[2] // 2
+
+    def taken(slabs, slot):
+        slab, place = slot // cap, slot % cap
+        value = slabs[0][place]
+        for d in range(1, n_slabs):
+            value = jnp.where(slab == d, slabs[d][place], value)
+        return value
+
     inner, outer = jnp.maximum(me - 1, 0), jnp.minimum(me + 1, n - 1)
     barrier = pltpu.get_barrier_semaphore()
 
@@ -41,9 +51,9 @@
 
     def segment(l, _):
         outside, inside = slot_ref[l * elems + 1], slot_ref[l * elems]
-        pair = blocks_ref[outside]
+        pair = taken(blocks, outside)
         inv, couple = pair[:, :size], pair[:, size:]
-        force = forcing_ref[outside]
+        force = taken(forces, outside)
         a_hi, a_lo = split(-dot(inv, couple))
         moved = dot(inv, force)
         moved = moved[:, :cols] + moved[:, cols:]
@@ -51,9 +61,9 @@
         first_lo[l] = a_lo
         first_shift[l] = moved
         f_hi, f_lo = split(moved)
-        pair = blocks_ref[inside]
+        pair = taken(blocks, inside)
         inv, couple = pair[:, :size], pair[:, size:]
-        force = forcing_ref[inside].astype(F32)
+        force = taken(forces, inside).astype(F32)
         force = force[:, :cols] + force[:, cols:]
         d_hi, d_lo = split(-(dot(couple, a_hi) + dot(couple, a_lo)))
         g_hi, g_lo = split(force - (dot(couple, f_hi) + dot(couple, f_lo)))
@@ -105,13 +115,13 @@
 
 
 def swept(n, lines, elems, slots, blocks, forcing):
-    size, cols = blocks.shape[1], forcing.shape[2] // 2
+    size, cols = blocks[0].shape[1], forcing[0].shape[2] // 2
     vmem = pl.BlockSpec(memory_space=pltpu.VMEM)
     square = pltpu.VMEM((lines, size, size), BF16)
     return pl.pallas_call(
-        functools.partial(line_kernel, n, lines, elems),
+        functools.partial(line_kernel, n, lines, elems, len(blocks)),
         out_shape=jax.ShapeDtypeStruct((lines, elems, size, cols), BF16),
-        in_specs=[pl.BlockSpec(memory_space=pltpu.SMEM), vmem, vmem],
+        in_specs=[pl.BlockSpec(memory_space=pltpu.SMEM)] + [vmem] * (2 * len(blocks)),
         out_specs=vmem,
         scratch_shapes=[
             square, square, square, square,
@@ -125,7 +135,7 @@
         compiler_params=pltpu.CompilerParams(
             collective_id=0, has_side_effects=True, vmem_limit_bytes=48 << 20
         ),
-    )(slots, blocks, forcing)
+    )(slots, *blocks, *forcing)
 
 
 def pack_kernel(pick_ref, inv_ref, couple_ref, out_ref):
@@ -200,17 +210,23 @@
     cols = rhs.shape[3]
     stored = lines * elems
     cap = send_list.shape[2]
-    total = n_surf * cap
     me = lax.axis_index("surf")
     ids = jnp.arange(cap, dtype=jnp.int32)[None, :]
     ranks = jnp.arange(n_surf, dtype=jnp.int32)
 
-    leaves = ids < send_count[0][:, None]
-    picks = jnp.where(leaves, send_list[0], 0).reshape(-1)
-    got_blocks = lax.all_to_all(
-        packed(picks, inv_block, couple_block).reshape(n_surf, cap, size, 2 * size),
-        "surf", split_axis=0, concat_axis=0, tiled=True,
-    )
+    onward = ranks[None] == ((me + ranks) % n_surf)[:, None]
+
+    def by_offset(rows):
+        return jnp.sum(jnp.where(onward[:, :, None], rows[None], 0), axis=1)
+
+    def moved(value, d):
+        return lax.ppermute(value, "surf", [(s, (s + d) % n_surf) for s in range(n_surf)])
+
+    leaves = ids < by_offset(send_count[0][:, None])
+    picks = jnp.where(leaves, by_offset(send_list[0]), 0)
+    order = sorted(range(n_surf), key=lambda d: -min(d, n_surf - d))
+    pairs = {d: packed(picks[d], inv_block, couple_block) for d in order}
+    got_blocks = [moved(pairs[d], d) if d else pairs[0] for d in range(n_surf)]
 
     table = jnp.concatenate([recv_list[0].reshape(-1), nb_line, send_count[0]])
     tables = lax.all_gather(table, "surf", axis=0, tiled=False)
@@ -219,29 +235,27 @@
     counts = tables[:, n_surf * cap + lines :]
 
     mine = jnp.sum(jnp.where((ranks == me)[None, :, None], places, 0), axis=1)
-    goal = jnp.where(leaves, mine + ranks[:, None] * stored, 0).reshape(-1)
+    goal = jnp.where(leaves, by_offset(mine + ranks[:, None] * stored), 0)
     goal_line, goal_elem = goal // elems, goal % elems
     all_lines = jnp.arange(n_surf * lines, dtype=jnp.int32)
-    nb = jnp.sum(jnp.where(goal_line[:, None] == all_lines[None], nb_all[None], 0), axis=1)
+    nb = jnp.sum(jnp.where(goal_line[..., None] == all_lines, nb_all, 0), axis=-1)
 
     lanes = jnp.concatenate([adjoint_prev[:, e] for e in range(elems)], axis=-1)
     adjoints = lax.all_gather(lanes, "surf", axis=0, tiled=True)
-    halves = forced(picks, nb, goal_elem, face_block, rhs, adjoints)
-    got_forcing = lax.all_to_all(
-        halves.reshape(n_surf, cap, size, 2 * cols), "surf", split_axis=0, concat_axis=0, tiled=True
-    )
+    later, _ = lax.optimization_barrier((picks, [pairs[d] for d in order]))
+    halves = {
+        d: forced(later[d], nb[d], goal_elem[d], face_block, rhs, adjoints) for d in order
+    }
+    got_forcing = [moved(halves[d], d) if d else halves[0] for d in range(n_surf)]
 
     to_me = jnp.sum(jnp.where((ranks == me)[None], counts, 0), axis=1)
     valid = (ids < to_me[:, None]).reshape(-1)
     positions = jnp.arange(stored, dtype=jnp.int32)
     hits = (recv_list[0].reshape(-1)[None] == positions[:, None]) & valid[None]
-    slots = jnp.sum(jnp.where(hits, jnp.arange(total, dtype=jnp.int32)[None], 0), axis=1)
-
-    return swept(
-        n_line, lines, elems, slots,
-        got_blocks.reshape(total, size, 2 * size),
-        got_forcing.reshape(total, size, 2 * cols),
-    )
+    places_here = ((me - ranks) % n_surf)[:, None] * cap + ids
+    slots = jnp.sum(jnp.where(hits, places_here.reshape(-1)[None], 0), axis=1)
+
+    return swept(n_line, lines, elems, slots, got_blocks, got_forcing)
 
 
 def solution(mesh):

time: 199 us -> 170 us (0.85)
  waiting for transfers between devices: 86.9 us -> 46.7 us
  Pallas kernels: 73.6 us -> 85.5 us
  local copies, waits for them, and re-layouts: 5.12 us -> 10.9 us
  starting transfers between devices: 8.87 us -> 3.54 us
    all_to_all x2 -> x0, waiting for transfers between devices: 77.8 us -> none  [the longest x1 73.2 us: per_device(): lax.all_to_all(packed(picks, inv_block, couple_block).reshape(n_surf, cap...]
    ppermute x0 -> x6, waiting for transfers between devices: none -> 46.7 us  [moved(): lax.ppermute(value, 'surf', [(s, (s + d) % n_surf) for s in range(n_surf)])]
    all_gather x1, waiting for transfers between devices: 9.15 us -> 0.01 us  [per_device(): adjoints = lax.all_gather(lanes, 'surf', axis=0, tiled=True)]
    all_to_all x2 -> x0, starting transfers between devices: 8.83 us -> none  [the longest x1 5.3 us: per_device(): lax.all_to_all(packed(picks, inv_block, couple_block).reshape(n_surf, cap...]
    pallas_call x1 -> x4, Pallas kernels: 13.7 us -> 19.5 us  [forced(): pl.pallas_call(functools.partial(force_kernel, elems), out_shape=jax.Shap...]
    pallas_call x1 -> x4, Pallas kernels: 12.7 us -> 17.6 us  [packed(): pl.pallas_call(pack_kernel, out_shape=jax.ShapeDtypeStruct((count, size,...]
    unnamed x17 -> x25, local copies, waits for them, and re-layouts: 2.23 us -> 5.85 us
    ppermute x0 -> x6, starting transfers between devices: none -> 3.5 us  [moved(): lax.ppermute(value, 'surf', [(s, (s + d) % n_surf) for s in range(n_surf)])]
  transfers between devices with their start and end apart: 3 -> 7, of which waited for: 3 -> 5; matrix products, arithmetic and copies ran while one was open for 3% -> 4% of each run, Pallas kernels for 6% -> 22%
where the time goes in v2:
time: 170 us; the launch traced here: 169 us
  Pallas kernels  85.5 us (50%)
  waiting for transfers between devices  46.7 us (27%)
  between operations  14.1 us (8%)
  local copies, waits for them, and re-layouts  10.9 us (6%)
  blocking collectives  6.38 us (4%)
  starting transfers between devices  3.54 us (2%)
  other arithmetic  2.36 us (1%)
    pallas_call x1, Pallas kernels, swept(): pl.pallas_call(functools.partial(line_kernel, n, lines, elems, len(blocks...  48.4 us
    ppermute x6, waiting for transfers between devices, moved(): lax.ppermute(value, 'surf', [(s, (s + d) % n_surf) for s in range(n_surf)])  46.7 us
    pallas_call x4, Pallas kernels, forced(): pl.pallas_call(functools.partial(force_kernel, elems), out_shape=jax.Shap...  19.5 us
    pallas_call x4, Pallas kernels, packed(): pl.pallas_call(pack_kernel, out_shape=jax.ShapeDtypeStruct((count, size,...  17.6 us
    unnamed x1, blocking collectives  6.38 us
    unnamed x25, local copies, waits for them, and re-layouts  5.85 us
    ppermute x6, starting transfers between devices, moved(): lax.ppermute(value, 'surf', [(s, (s + d) % n_surf) for s in range(n_surf)])  3.5 us
  transfers between devices with their start and end apart: 7, of which 5 were waited for; matrix products, arithmetic and copies ran while one was open for 4% of the time, Pallas kernels for 22%

profile of v2, /device:TPU:0, one launch (start us, length us, event | category | flops | bytes accessed | tf_op | source)
XLA Modules:
  0.0 169.5 jit_solution(12420865404168548340)
XLA Ops:
  6.6 1.1 fusion.7
  8.1 0.9 pad_maximum_fusion
  10.9 6.4 %all-reduce = s32[96]{0:T(128)S(1)} all-reduce(s32[96]{0:T(128)S(1)} %add_dynamic-update-slice_fusion), channel_id=2, replica_groups=mesh['surf'=4,'line'=8] {'surf'}, use_global_device_ids=true, to_apply=%add | all-reduce | flops 96 | bytes 768
  18.4 4.5 %shard_map.92 = bf16[4,320,640]{2,1,0:T(8,128)(2,1)} custom-call(s32[4]{0:T(128)} %get-tuple-element.29.pick_ref, bf16[4,2,320,320]{3,2,1,0:T(8,128)(2,1)} %inv_ref.7, bf16[4,2,320,320]{3,2,1,0:T(8,128)(2,1)} %couple_ref.7), custom_call_target="tpu_custom_call" | custom-call | bytes 3276800 | tf_op jit(solution)/shard_map/pallas_call | solution.py:153
  22.9 3.8 %shard_map.93 = bf16[4,320,640]{2,1,0:T(8,128)(2,1)} custom-call(s32[4]{0:T(128)} %get-tuple-element.28.pick_ref, bf16[4,2,320,320]{3,2,1,0:T(8,128)(2,1)} %inv_ref.7, bf16[4,2,320,320]{3,2,1,0:T(8,128)(2,1)} %couple_ref.7), custom_call_target="tpu_custom_call" | custom-call | bytes 3276800 | tf_op jit(solution)/shard_map/pallas_call | solution.py:153
  27.6 4.8 %shard_map.94 = bf16[4,320,640]{2,1,0:T(8,128)(2,1)} custom-call(s32[4]{0:T(128)} %get-tuple-element.27.pick_ref, bf16[4,2,320,320]{3,2,1,0:T(8,128)(2,1)} %inv_ref.7, bf16[4,2,320,320]{3,2,1,0:T(8,128)(2,1)} %couple_ref.7), custom_call_target="tpu_custom_call" | custom-call | bytes 3276800 | tf_op jit(solution)/shard_map/pallas_call | solution.py:153
  32.4 1.5 collective-permute-start.2
  34.3 1.1 copy.26.rhs_ref
  35.4 4.4 %shard_map.91.refs_0_ = bf16[4,320,640]{2,1,0:T(8,128)(2,1)} custom-call(s32[4]{0:T(128)} %get-tuple-element.30.pick_ref, bf16[4,2,320,320]{3,2,1,0:T(8,128)(2,1)} %inv_ref.7, bf16[4,2,320,320]{3,2,1,0:T(8,128)(2,1)} %couple_ref.7), custom_call_target="tpu_custom_call" | custom-call | bytes 3276800 | tf_op jit(solution)/shard_map/pallas_call | solution.py:153
  41.9 4.9 %shard_map.96 = bf16[4,320,128]{2,1,0:T(8,128)(2,1)} custom-call(s32[4]{0:T(128)} %get-tuple-element.23.pick_ref, s32[4]{0:T(128)} %get-tuple-element.19.line_ref, s32[4]{0:T(128)} %get-tuple-element.15.elem_ref, bf16[4,2,320,320]{3,2,1,0:T(8,128)(2,1)} %face_ref.7, bf16[4,2,320,64]{3,2,1,0:T(8,128)(2,1)} %copy.26.rhs_ref, ...), custom_call_target="tpu_custom_call" | custom-call | flops 104857600 | bytes 819200 | tf_op jit(solution)/shard_map/pallas_call | solution.py:187
  46.8 4.5 %shard_map.97 = bf16[4,320,128]{2,1,0:T(8,128)(2,1)} custom-call(s32[4]{0:T(128)} %get-tuple-element.22.pick_ref, s32[4]{0:T(128)} %get-tuple-element.18.line_ref, s32[4]{0:T(128)} %get-tuple-element.14.elem_ref, bf16[4,2,320,320]{3,2,1,0:T(8,128)(2,1)} %face_ref.7, bf16[4,2,320,64]{3,2,1,0:T(8,128)(2,1)} %copy.26.rhs_ref, ...), custom_call_target="tpu_custom_call" | custom-call | flops 104857600 | bytes 819200 | tf_op jit(solution)/shard_map/pallas_call | solution.py:187
  51.3 1.2 collective-permute-start.4
  52.5 5.0 %shard_map.98 = bf16[4,320,128]{2,1,0:T(8,128)(2,1)} custom-call(s32[4]{0:T(128)} %get-tuple-element.21.pick_ref, s32[4]{0:T(128)} %get-tuple-element.17.line_ref, s32[4]{0:T(128)} %get-tuple-element.13.elem_ref, bf16[4,2,320,320]{3,2,1,0:T(8,128)(2,1)} %face_ref.7, bf16[4,2,320,64]{3,2,1,0:T(8,128)(2,1)} %copy.26.rhs_ref, ...), custom_call_target="tpu_custom_call" | custom-call | flops 104857600 | bytes 819200 | tf_op jit(solution)/shard_map/pallas_call | solution.py:187
  57.5 4.3 %collective-permute-done.refs_1_ = bf16[4,320,640]{2,1,0:T(8,128)(2,1)S(1)} collective-permute-done((bf16[4,320,640]{2,1,0:T(8,128)(2,1)}, bf16[4,320,640]{2,1,0:T(8,128)(2,1)S(1)}, u32[]{:S(2)}, u32[]{:S(2)}) %collective-permute-start) | collective-permute-done | bytes 1638432 | tf_op jit(solution)/shard_map/ppermute | solution.py:223
  61.8 1.3 copy-done.1
  63.4 5.1 %shard_map.95.refs_4_ = bf16[4,320,128]{2,1,0:T(8,128)(2,1)} custom-call(s32[4]{0:T(128)} %get-tuple-element.24.pick_ref, s32[4]{0:T(128)} %get-tuple-element.20.line_ref, s32[4]{0:T(128)} %get-tuple-element.16.elem_ref, bf16[4,2,320,320]{3,2,1,0:T(8,128)(2,1)} %face_ref.7, bf16[4,2,320,64]{3,2,1,0:T(8,128)(2,1)} %copy.26.rhs_ref, ...), custom_call_target="tpu_custom_call" | custom-call | flops 104857600 | bytes 819200 | tf_op jit(solution)/shard_map/pallas_call | solution.py:187
  68.4 30.8 %collective-permute-done.2.refs_3_ = bf16[4,320,640]{2,1,0:T(8,128)(2,1)} collective-permute-done((bf16[4,320,640]{2,1,0:T(8,128)(2,1)}, bf16[4,320,640]{2,1,0:T(8,128)(2,1)}, u32[]{:S(2)}, u32[]{:S(2)}) %collective-permute-start.2) | collective-permute-done | bytes 1638432 | tf_op jit(solution)/shard_map/ppermute | solution.py:223
  99.3 4.7 %collective-permute-done.3.refs_5_ = bf16[4,320,128]{2,1,0:T(8,128)(2,1)S(1)} collective-permute-done((bf16[4,320,128]{2,1,0:T(8,128)(2,1)}, bf16[4,320,128]{2,1,0:T(8,128)(2,1)S(1)}, u32[]{:S(2)}, u32[]{:S(2)}) %collective-permute-start.3) | collective-permute-done | bytes 327712 | tf_op jit(solution)/shard_map/ppermute | solution.py:223
  103.9 3.9 %collective-permute-done.4.refs_6_ = bf16[4,320,128]{2,1,0:T(8,128)(2,1)S(1)} collective-permute-done((bf16[4,320,128]{2,1,0:T(8,128)(2,1)}, bf16[4,320,128]{2,1,0:T(8,128)(2,1)S(1)}, u32[]{:S(2)}, u32[]{:S(2)}) %collective-permute-start.4) | collective-permute-done | bytes 327712 | tf_op jit(solution)/shard_map/ppermute | solution.py:223
  107.8 3.0 %collective-permute-done.5.refs_7_ = bf16[4,320,128]{2,1,0:T(8,128)(2,1)S(1)} collective-permute-done((bf16[4,320,128]{2,1,0:T(8,128)(2,1)}, bf16[4,320,128]{2,1,0:T(8,128)(2,1)S(1)}, u32[]{:S(2)}, u32[]{:S(2)}) %collective-permute-start.5) | collective-permute-done | bytes 327712 | tf_op jit(solution)/shard_map/ppermute | solution.py:223
  110.8 1.4 copy-done.2
  112.3 1.0 copy-done.3
  113.2 48.4 %shard_map.99 = bf16[4,2,320,64]{3,2,1,0:T(8,128)(2,1)S(1)} custom-call(s32[8]{0:T(128)S(1)} %select_reduce_fusion.4.slot_ref, bf16[4,320,640]{2,1,0:T(8,128)(2,1)S(1)} %copy-done, bf16[4,320,640]{2,1,0:T(8,128)(2,1)S(1)} %copy-done.2, bf16[4,320,640]{2,1,0:T(8,128)(2,1)} %collective-permute-done.1.refs_2_, ...), custom_call_target="tpu_custom_call" | custom-call | tf_op jit(solution)/shard_map/pallas_call | solution.py:121
  161.6 1.0 copy.30
  (54 shorter events, 6.3 us)
Async XLA Ops:
  6.5 3.0 %copy-start.9 = (u32[32]{0:T(128)S(1)}, u32[32]{0:T(128)}, u32[]{:S(2)}) copy-start(u32[32]{0:T(128)} %constant.64) | copy-start | bytes 388
  6.5 2.6 %copy-start.6 = (s32[1,4,4]{2,1,0:T(4,128)S(1)}, s32[1,4,4]{2,1,0:T(4,128)}, u32[]{:S(2)}) copy-start(s32[1,4,4]{2,1,0:T(4,128)} %param.17) | copy-start | bytes 196
  6.5 2.8 %copy-start.7 = (s32[1,4]{1,0:T(1,128)S(1)}, s32[1,4]{1,0:T(1,128)}, u32[]{:S(2)}) copy-start(s32[1,4]{1,0:T(1,128)} %param.16) | copy-start | bytes 52
  6.5 4.2 %copy-start.8 = (s32[4]{0:T(128)S(1)}, s32[4]{0:T(128)}, u32[]{:S(2)}) copy-start(s32[4]{0:T(128)} %param.14) | copy-start | bytes 52
  6.5 11.1 %copy-start.5 = (s32[1,4,4]{2,1,0:T(4,128)S(1)}, s32[1,4,4]{2,1,0:T(4,128)}, u32[]{:S(2)}) copy-start(s32[1,4,4]{2,1,0:T(4,128)} %param.15) | copy-start | bytes 196
  6.5 35.3 %all-gather.3.cloned.1.call-start = ((), (), s32[]{:S(2)}) async-start(), calls=%async_computation | async-start | bytes 1638400 | tf_op jit(solution)/shard_map/all_gather | solution.py:244
  22.9 38.9 %collective-permute-start = (bf16[4,320,640]{2,1,0:T(8,128)(2,1)}, bf16[4,320,640]{2,1,0:T(8,128)(2,1)S(1)}, u32[]{:S(2)}, u32[]{:S(2)}) collective-permute-start(bf16[4,320,640]{2,1,0:T(8,128)(2,1)} %shard_map.92), channel_id=1, source_target_pairs={{0,8},{8,16},{16,24},{24,0},{1,9},{9,17},{17,25},{25,1},{2,10},{10... | collective-permute-start | bytes 4915208 | tf_op jit(solution)/shard_map/ppermute | solution.py:223
  26.7 41.7 %collective-permute-start.1 = (bf16[4,320,640]{2,1,0:T(8,128)(2,1)}, bf16[4,320,640]{2,1,0:T(8,128)(2,1)}, u32[]{:S(2)}, u32[]{:S(2)}) collective-permute-start(bf16[4,320,640]{2,1,0:T(8,128)(2,1)} %shard_map.93), channel_id=1, source_target_pairs={{0,16},{8,24},{16,0},{24,8},{1,17},{9,25},{17,1},{25,9},{2,18},{10... | collective-permute-start | bytes 4915208 | tf_op jit(solution)/shard_map/ppermute | solution.py:223
  27.6 6.7 %copy-start.4 = (bf16[4,2,320,64]{2,3,1,0:T(8,128)(2,1)S(1)}, bf16[4,2,320,64]{2,3,1,0:T(8,128)(2,1)}, u32[]{:S(2)}) copy-start(bf16[4,2,320,64]{2,3,1,0:T(8,128)(2,1)} %param.12) | copy-start | bytes 983044
  32.4 66.8 %collective-permute-start.2 = (bf16[4,320,640]{2,1,0:T(8,128)(2,1)}, bf16[4,320,640]{2,1,0:T(8,128)(2,1)}, u32[]{:S(2)}, u32[]{:S(2)}) collective-permute-start(bf16[4,320,640]{2,1,0:T(8,128)(2,1)} %shard_map.94), channel_id=1, source_target_pairs={{0,24},{8,0},{16,8},{24,16},{1,25},{9,1},{17,9},{25,17},{2,26},{10... | collective-permute-start | bytes 4915208 | tf_op jit(solution)/shard_map/ppermute | solution.py:223
  46.8 57.1 %collective-permute-start.3 = (bf16[4,320,128]{2,1,0:T(8,128)(2,1)}, bf16[4,320,128]{2,1,0:T(8,128)(2,1)S(1)}, u32[]{:S(2)}, u32[]{:S(2)}) collective-permute-start(bf16[4,320,128]{2,1,0:T(8,128)(2,1)} %shard_map.96), channel_id=1, source_target_pairs={{0,8},{8,16},{16,24},{24,0},{1,9},{9,17},{17,25},{25,1},{2,10},{10... | collective-permute-start | bytes 983048 | tf_op jit(solution)/shard_map/ppermute | solution.py:223
  51.3 56.5 %collective-permute-start.4 = (bf16[4,320,128]{2,1,0:T(8,128)(2,1)}, bf16[4,320,128]{2,1,0:T(8,128)(2,1)S(1)}, u32[]{:S(2)}, u32[]{:S(2)}) collective-permute-start(bf16[4,320,128]{2,1,0:T(8,128)(2,1)} %shard_map.97), channel_id=1, source_target_pairs={{0,16},{8,24},{16,0},{24,8},{1,17},{9,25},{17,1},{25,9},{2,18},{10... | collective-permute-start | bytes 983048 | tf_op jit(solution)/shard_map/ppermute | solution.py:223
  61.8 1.3 copy-start.1
  63.1 47.8 %collective-permute-start.5 = (bf16[4,320,128]{2,1,0:T(8,128)(2,1)}, bf16[4,320,128]{2,1,0:T(8,128)(2,1)S(1)}, u32[]{:S(2)}, u32[]{:S(2)}) collective-permute-start(bf16[4,320,128]{2,1,0:T(8,128)(2,1)} %shard_map.98), channel_id=1, source_target_pairs={{0,24},{8,0},{16,8},{24,16},{1,25},{9,1},{17,9},{25,17},{2,26},{10... | collective-permute-start | bytes 983048 | tf_op jit(solution)/shard_map/ppermute | solution.py:223
  63.4 47.5 %copy-start = (bf16[4,320,640]{2,1,0:T(8,128)(2,1)S(1)}, bf16[4,320,640]{2,1,0:T(8,128)(2,1)}, u32[]{:S(2)}) copy-start(bf16[4,320,640]{2,1,0:T(8,128)(2,1)} %shard_map.91.refs_0_) | copy-start | bytes 4915204
  110.8 1.4 copy-start.2
  112.3 1.0 copy-start.3
Sparse Core Ops, SparseCore 0:
  9.2 22.2 all-gather.2
